TPU v7x, 512 devices: a whole 4x8x8 slice. The times are simulated.
512 devices in a mesh: dp: 64 (over x, z, core), mp: 8 (over y).
Axes of the slice: x: 4, y: 8, z: 8, core: 2. Of those that a mesh axis runs over, the one named last changes fastest.
Arguments:
- child_queries: bfloat16 [64, 4, 128, 64, 128], P('dp', None, None, 'mp'), may hold values from -72 to 72
- child_keys: bfloat16 [64, 4, 128, 8, 128], P('dp', None, None, 'mp'), may hold values from -5 to 5
- child_values: bfloat16 [64, 4, 128, 8, 128], P('dp', None, None, 'mp'), may hold values from -36 to 36
- prefix_keys: bfloat16 [64, 2048, 8, 128], P('dp', None, 'mp'), may hold values from -6.25 to 6.25
- prefix_values: bfloat16 [64, 2048, 8, 128], P('dp', None, 'mp'), may hold values from -36 to 36
- child_count: int32 [64], P('dp'), may hold values from 1 to 4, as said below
- child_parent: int32 [64, 4], P('dp'), may hold values from 0 to 63, as said below
- reward_weight: bfloat16 [64, 128, 2], P('mp'), may hold values from -0.14941406 to 0.14941406
Outputs:
- attended: bfloat16 [64, 4, 128, 64, 128], P('dp', None, None, 'mp')
- reward_logits: float32 [64, 4, 128, 2], P('dp')
Inputs may be any that keep to these rules, and one draw needn't show every extreme that they name: `child_count`: 4 is reached on some index of dp in every draw. `child_parent`: the parent of a child in row p is one of p, p - 1, ..., p - 3, taken modulo 64.
All inputs are finite; a program needn't handle non-finite values.
Results may differ from a plain program's by a relative error of at most 0.014.
Values may be sent and summed in bfloat16 or wider, within the bound.
A program may use at most 128 MiB of HBM per device.

v0:
```python
import jax
import jax.numpy as jnp
from jax import lax
from jax.sharding import PartitionSpec as P

WINDOW = 4


neg_large = -1e30


def passed_along(value, axis, steps):
    count = lax.axis_size(axis)
    pairs = [(source, (source + steps) % count) for source in range(count)]
    return lax.ppermute(value, axis, pairs)


def attend_part(query_block, key_rows, value_rows, causal):
    query_rows, heads_here, head_size = query_block.shape
    kv_heads = key_rows.shape[1]
    grouped = query_block.reshape(query_rows, kv_heads, heads_here // kv_heads, head_size)
    scores = jnp.einsum(
        "tkgd,skd->kgts", grouped, key_rows, preferred_element_type=jnp.float32
    ) * head_size ** (-0.5)
    if causal:
        row_iota = lax.broadcasted_iota(jnp.int32, (query_rows, key_rows.shape[0]), 0)
        col_iota = lax.broadcasted_iota(jnp.int32, (query_rows, key_rows.shape[0]), 1)
        scores = jnp.where(col_iota <= row_iota, scores, neg_large)
    row_peak = jnp.max(scores, axis=-1)
    weights = jnp.exp(scores - row_peak[..., None])
    row_total = jnp.sum(weights, axis=-1)
    weighted = jnp.einsum(
        "kgts,skd->tkgd",
        weights.astype(jnp.bfloat16),
        value_rows,
        preferred_element_type=jnp.float32,
    )
    return (row_peak, row_total, weighted)


def to_rows(stat):
    return jnp.transpose(stat, (2, 0, 1))[..., None]


def combine_parts(first, second):
    row_peak = jnp.maximum(first[0], second[0])
    first_scale = jnp.exp(first[0] - row_peak)
    second_scale = jnp.exp(second[0] - row_peak)
    row_total = first[1] * first_scale + second[1] * second_scale
    weighted = first[2] * to_rows(first_scale) + second[2] * to_rows(second_scale)
    normed = weighted / to_rows(row_total)
    query_rows, kv_heads, groups, head_size = normed.shape
    return normed.reshape(query_rows, kv_heads * groups, head_size).astype(jnp.bfloat16)


def shards(
    child_queries,
    child_keys,
    child_values,
    prefix_keys,
    prefix_values,
    child_count,
    child_parent,
    reward_weight,
):
    devices = lax.axis_size("dp")
    position = lax.axis_index("dp")
    queries = child_queries[0]
    own_keys = child_keys[0]
    own_values = child_values[0]
    capacity, query_rows, heads_here, head_size = queries.shape
    slot_ids = jnp.arange(capacity, dtype=jnp.int32)
    active = slot_ids < child_count[0]
    distance = jnp.mod(position - child_parent[0], devices)
    empty_out = jnp.zeros((query_rows, heads_here, head_size), jnp.bfloat16)
    key_list = [prefix_keys[0]]
    value_list = [prefix_values[0]]
    for offset in range(1, WINDOW):
        got_keys, got_values = passed_along((prefix_keys, prefix_values), "dp", offset)
        key_list.append(got_keys[0])
        value_list.append(got_values[0])
    key_stack = jnp.stack(key_list)
    value_stack = jnp.stack(value_list)

    def finish(member):
        parent_keys = lax.dynamic_index_in_dim(key_stack, distance[member], 0, keepdims=False)
        parent_values = lax.dynamic_index_in_dim(value_stack, distance[member], 0, keepdims=False)
        prefix_part = attend_part(queries[member], parent_keys, parent_values, False)
        own_part = attend_part(queries[member], own_keys[member], own_values[member], True)
        return combine_parts(prefix_part, own_part)

    def vacant(member):
        return empty_out

    def guarded(member):
        return lax.cond(active[member], finish, vacant, member)

    attended = lax.map(guarded, slot_ids)
    partial_logits = jnp.einsum(
        "cthd,hdz->ctz", attended, reward_weight, preferred_element_type=jnp.float32
    )
    logits = lax.psum(partial_logits, "mp")
    return (attended[None], logits[None])


def solution(mesh):
    placed = (
        P("dp", None, None, "mp", None),
        P("dp", None, None, "mp", None),
        P("dp", None, None, "mp", None),
        P("dp", None, "mp", None),
        P("dp", None, "mp", None),
        P("dp"),
        P("dp", None),
        P("mp", None, None),
    )
    return jax.shard_map(
        shards,
        mesh=mesh,
        in_specs=placed,
        out_specs=(P("dp", None, None, "mp", None), P("dp", None, None, None)),
        check_vma=False,
    )
```

profile of v0, /device:TPU:448, one launch (start us, length us, event | category | flops | bytes accessed | tf_op | source)
XLA Modules:
  0.0 159.7 jit_solution(9125864456757356966)
XLA Ops:
  2.0 1.9 %collective-permute-start = (bf16[1,2048,1,128]{1,3,2,0:T(8,128)(2,1)S(1)}, bf16[1,2048,1,128]{1,3,2,0:T(8,128)(2,1)S(1)}, u32[]{:S(2)}, u32[]{:S(2)}) collective-permute-start(bf16[1,2048,1,128]{1,3,2,0:T(8,128)(2,1)S(1)} %copy.15), channel_id=1, source_target_pairs={{0,8},{8,16},{16,24},{24,32},{32,40},{40,48},{48,56},{56,64},{64,7... | collective-permute-start | bytes 1572872 | tf_op jit(solution)/shard_map/ppermute | solution.py:15
  3.9 1.9 %collective-permute-start.1 = (bf16[1,2048,1,128]{1,3,2,0:T(8,128)(2,1)S(1)}, bf16[1,2048,1,128]{1,3,2,0:T(8,128)(2,1)S(1)}, u32[]{:S(2)}, u32[]{:S(2)}) collective-permute-start(bf16[1,2048,1,128]{1,3,2,0:T(8,128)(2,1)S(1)} %copy.15), channel_id=1, source_target_pairs={{0,16},{8,24},{16,32},{24,40},{32,48},{40,56},{48,64},{56,72},{64,... | collective-permute-start | bytes 1572872 | tf_op jit(solution)/shard_map/ppermute | solution.py:15
  5.8 1.9 %collective-permute-start.2 = (bf16[1,2048,1,128]{1,3,2,0:T(8,128)(2,1)S(1)}, bf16[1,2048,1,128]{1,3,2,0:T(8,128)(2,1)}, u32[]{:S(2)}, u32[]{:S(2)}) collective-permute-start(bf16[1,2048,1,128]{1,3,2,0:T(8,128)(2,1)S(1)} %copy.15), channel_id=1, source_target_pairs={{0,24},{8,32},{16,40},{24,48},{32,56},{40,64},{48,72},{56,80},{64,... | collective-permute-start | bytes 1572872 | tf_op jit(solution)/shard_map/ppermute | solution.py:15
  7.7 1.9 %collective-permute-start.3 = (bf16[1,2048,1,128]{3,1,2,0:T(8,128)(2,1)}, bf16[1,2048,1,128]{3,1,2,0:T(8,128)(2,1)}, u32[]{:S(2)}, u32[]{:S(2)}) collective-permute-start(bf16[1,2048,1,128]{3,1,2,0:T(8,128)(2,1)} %param.15), channel_id=1, source_target_pairs={{0,8},{8,16},{16,24},{24,32},{32,40},{40,48},{48,56},{56,64},{64,7... | collective-permute-start | bytes 1572872 | tf_op jit(solution)/shard_map/ppermute | solution.py:15
  9.7 3.7 %collective-permute-start.4 = (bf16[1,2048,1,128]{3,1,2,0:T(8,128)(2,1)}, bf16[1,2048,1,128]{3,1,2,0:T(8,128)(2,1)}, u32[]{:S(2)}, u32[]{:S(2)}) collective-permute-start(bf16[1,2048,1,128]{3,1,2,0:T(8,128)(2,1)} %param.15), channel_id=1, source_target_pairs={{0,16},{8,24},{16,32},{24,40},{32,48},{40,56},{48,64},{56,72},{64,... | collective-permute-start | bytes 1572872 | tf_op jit(solution)/shard_map/ppermute | solution.py:15
  16.3 4.8 %collective-permute-start.5 = (bf16[1,2048,1,128]{3,1,2,0:T(8,128)(2,1)}, bf16[1,2048,1,128]{3,1,2,0:T(8,128)(2,1)}, u32[]{:S(2)}, u32[]{:S(2)}) collective-permute-start(bf16[1,2048,1,128]{3,1,2,0:T(8,128)(2,1)} %param.15), channel_id=1, source_target_pairs={{0,24},{8,32},{16,40},{24,48},{32,56},{40,64},{48,72},{56,80},{64,... | collective-permute-start | bytes 1572872 | tf_op jit(solution)/shard_map/ppermute | solution.py:15
  23.6 20.1 %collective-permute-done.2 = bf16[1,2048,1,128]{1,3,2,0:T(8,128)(2,1)} collective-permute-done((bf16[1,2048,1,128]{1,3,2,0:T(8,128)(2,1)S(1)}, bf16[1,2048,1,128]{1,3,2,0:T(8,128)(2,1)}, u32[]{:S(2)}, u32[]{:S(2)}) %collective-permute-start.2) | collective-permute-done | bytes 524320 | tf_op jit(solution)/shard_map/ppermute | solution.py:15
  43.7 1.8 %pad_maximum_fusion = bf16[4,2048,1,128]{1,3,2,0:T(8,128)(2,1)S(1)} fusion(bf16[1,2048,1,128]{1,3,2,0:T(8,128)(2,1)} %collective-permute-done.2, bf16[1,2048,1,128]{1,3,2,0:T(8,128)(2,1)} %copy-done.5, bf16[1,2048,1,128]{1,3,2,0:T(8,128)(2,1)} %copy-done.4, bf16[1,2048,1,128]{1,3,2,0:T(8,128)(2,1)} %copy-done.2), kind=kLoop, calls=%fused_computation.53 | loop fusion | flops 3145728 | bytes 4194304 | tf_op jit(solution)/shard_map/stack | solution.py:83
  45.5 9.5 %collective-permute-done.3 = bf16[1,2048,1,128]{3,1,2,0:T(8,128)(2,1)} collective-permute-done((bf16[1,2048,1,128]{3,1,2,0:T(8,128)(2,1)}, bf16[1,2048,1,128]{3,1,2,0:T(8,128)(2,1)}, u32[]{:S(2)}, u32[]{:S(2)}) %collective-permute-start.3) | collective-permute-done | bytes 524320 | tf_op jit(solution)/shard_map/ppermute | solution.py:15
  54.9 19.4 %collective-permute-done.5 = bf16[1,2048,1,128]{3,1,2,0:T(8,128)(2,1)} collective-permute-done((bf16[1,2048,1,128]{3,1,2,0:T(8,128)(2,1)}, bf16[1,2048,1,128]{3,1,2,0:T(8,128)(2,1)}, u32[]{:S(2)}, u32[]{:S(2)}) %collective-permute-start.5) | collective-permute-done | bytes 524320 | tf_op jit(solution)/shard_map/ppermute | solution.py:15
  74.4 3.0 %pad_maximum_fusion.1 = bf16[4,2048,1,128]{3,1,2,0:T(8,128)(2,1)} fusion(bf16[1,2048,1,128]{3,1,2,0:T(8,128)(2,1)} %collective-permute-done.5, bf16[1,2048,1,128]{3,1,2,0:T(8,128)(2,1)} %collective-permute-done.4, bf16[1,2048,1,128]{3,1,2,0:T(8,128)(2,1)} %collective-permute-done.3, bf16[1,2048,1,128]{3,1,2,0:T(8,128)(2,1)S(1)} %copy-done.3), kind=kLoop, calls=%fused_computation.54 | loop fusion | flops 3145728 | bytes 4194304 | tf_op jit(solution)/shard_map/stack | solution.py:82
  77.3 61.5 %while.10 = (s32[]{:T(128)}, bf16[4,128,8,128]{1,3,2,0:T(8,128)(2,1)}, s32[4]{0:T(128)S(1)}, pred[4]{0:T(512)(128)(4,1)S(1)}, s32[4]{0:T(128)S(1)}, /*index=5*/b...) while((s32[]{:T(128)}, ...), condition=%wide.region_7.8_spmd, body=%wide.region_0.7_spmd.sunk | while | flops 1159219200 | bytes 30320468 | solution.py:98
  81.0 10.9 %conditional.2 = (bf16[1,128,8,128]{1,3,2,0:T(8,128)(2,1)S(1)}) conditional(s32[]{:T(128)} %bitcast.156, () %tuple.36, (s32[]{:T(128)}, s32[4]{0:T(128)S(1)}, bf16[4,2048,1,128]{1,3,2,0:T(8,128)(2,1)S(1)}, bf16[4,2048,1,128]{3,1,2,0:T(8,128)(2,1)}, bf16[4,128,8,128]{3,1,2,0:T(8,128)(2,1)S(1)}, /*index=5*/bf16[4,128,1,128]{3,1,2,0:T(8,128)(2,1)}, ...), branch_computations={%region_1.1_spmd, %region_2.6_spmd} | conditional | flops 1159219200 | bytes 29795432 | solution.py:96
  85.2 2.3 %bitcast_reduce_fusion = (f32[8,128]{1,0:T(8,128)S(1)}, f32[2048,128,8]{1,0,2:T(8,128)S(1)}) fusion(bf16[4,128,8,128]{3,1,2,0:T(8,128)(2,1)S(1)} %get-tuple-element.62, s32[]{:T(128)S(6)} %select_n.22, bf16[4,2048,1,128]{3,1,2,0:T(8,128)(2,1)} %get-tuple-element.61, s32[]{:T(128)S(6)} %select_n.23), kind=kOutput, calls=%fused_computation.1 | convolution fusion | flops 541064192 | bytes 9179144 | tf_op jit(solution)/shard_map/while/body/eval_jaxpr/cond/branch_1_fun/tkgd,skd->kgts/dot_general | solution.py:22
  90.1 1.6 %fusion.13 = f32[128,1,8,128]{0,3,2,1:T(8,128)S(1)} fusion(f32[2048,128,8]{1,0,2:T(8,128)S(1)} %get-tuple-element.104, f32[8,128]{1,0:T(8,128)S(1)} %get-tuple-element.103, bf16[4,2048,1,128]{1,3,2,0:T(8,128)(2,1)S(1)} %get-tuple-element.58, s32[]{:T(128)S(6)} %select_n.23, f32[128,8]{0,1:T(8,128)S(1)} %get-tuple-element.102), kind=kOutput, calls=%fused_computation.14 | convolution fusion | flops 543293440 | bytes 9445380 | tf_op jit(solution)/shard_map/while/body/eval_jaxpr/cond/branch_1_fun/kgts,skd->tkgd/dot_general | solution.py:32
  96.4 10.9 %conditional.2 = (bf16[1,128,8,128]{1,3,2,0:T(8,128)(2,1)S(1)}) conditional(s32[]{:T(128)} %bitcast.156, () %tuple.36, (s32[]{:T(128)}, s32[4]{0:T(128)S(1)}, bf16[4,2048,1,128]{1,3,2,0:T(8,128)(2,1)S(1)}, bf16[4,2048,1,128]{3,1,2,0:T(8,128)(2,1)}, bf16[4,128,8,128]{3,1,2,0:T(8,128)(2,1)S(1)}, /*index=5*/bf16[4,128,1,128]{3,1,2,0:T(8,128)(2,1)}, ...), branch_computations={%region_1.1_spmd, %region_2.6_spmd} | conditional | flops 1159219200 | bytes 29795432 | solution.py:96
  100.6 2.3 %bitcast_reduce_fusion = (f32[8,128]{1,0:T(8,128)S(1)}, f32[2048,128,8]{1,0,2:T(8,128)S(1)}) fusion(bf16[4,128,8,128]{3,1,2,0:T(8,128)(2,1)S(1)} %get-tuple-element.62, s32[]{:T(128)S(6)} %select_n.22, bf16[4,2048,1,128]{3,1,2,0:T(8,128)(2,1)} %get-tuple-element.61, s32[]{:T(128)S(6)} %select_n.23), kind=kOutput, calls=%fused_computation.1 | convolution fusion | flops 541064192 | bytes 9179144 | tf_op jit(solution)/shard_map/while/body/eval_jaxpr/cond/branch_1_fun/tkgd,skd->kgts/dot_general | solution.py:22
  111.7 10.9 %conditional.2 = (bf16[1,128,8,128]{1,3,2,0:T(8,128)(2,1)S(1)}) conditional(s32[]{:T(128)} %bitcast.156, () %tuple.36, (s32[]{:T(128)}, s32[4]{0:T(128)S(1)}, bf16[4,2048,1,128]{1,3,2,0:T(8,128)(2,1)S(1)}, bf16[4,2048,1,128]{3,1,2,0:T(8,128)(2,1)}, bf16[4,128,8,128]{3,1,2,0:T(8,128)(2,1)S(1)}, /*index=5*/bf16[4,128,1,128]{3,1,2,0:T(8,128)(2,1)}, ...), branch_computations={%region_1.1_spmd, %region_2.6_spmd} | conditional | flops 1159219200 | bytes 29795432 | solution.py:96
  116.0 2.3 %bitcast_reduce_fusion = (f32[8,128]{1,0:T(8,128)S(1)}, f32[2048,128,8]{1,0,2:T(8,128)S(1)}) fusion(bf16[4,128,8,128]{3,1,2,0:T(8,128)(2,1)S(1)} %get-tuple-element.62, s32[]{:T(128)S(6)} %select_n.22, bf16[4,2048,1,128]{3,1,2,0:T(8,128)(2,1)} %get-tuple-element.61, s32[]{:T(128)S(6)} %select_n.23), kind=kOutput, calls=%fused_computation.1 | convolution fusion | flops 541064192 | bytes 9179144 | tf_op jit(solution)/shard_map/while/body/eval_jaxpr/cond/branch_1_fun/tkgd,skd->kgts/dot_general | solution.py:22
  120.8 1.6 %fusion.13 = f32[128,1,8,128]{0,3,2,1:T(8,128)S(1)} fusion(f32[2048,128,8]{1,0,2:T(8,128)S(1)} %get-tuple-element.104, f32[8,128]{1,0:T(8,128)S(1)} %get-tuple-element.103, bf16[4,2048,1,128]{1,3,2,0:T(8,128)(2,1)S(1)} %get-tuple-element.58, s32[]{:T(128)S(6)} %select_n.23, f32[128,8]{0,1:T(8,128)S(1)} %get-tuple-element.102), kind=kOutput, calls=%fused_computation.14 | convolution fusion | flops 543293440 | bytes 9445380 | tf_op jit(solution)/shard_map/while/body/eval_jaxpr/cond/branch_1_fun/kgts,skd->tkgd/dot_general | solution.py:32
  127.1 10.9 %conditional.2 = (bf16[1,128,8,128]{1,3,2,0:T(8,128)(2,1)S(1)}) conditional(s32[]{:T(128)} %bitcast.156, () %tuple.36, (s32[]{:T(128)}, s32[4]{0:T(128)S(1)}, bf16[4,2048,1,128]{1,3,2,0:T(8,128)(2,1)S(1)}, bf16[4,2048,1,128]{3,1,2,0:T(8,128)(2,1)}, bf16[4,128,8,128]{3,1,2,0:T(8,128)(2,1)S(1)}, /*index=5*/bf16[4,128,1,128]{3,1,2,0:T(8,128)(2,1)}, ...), branch_computations={%region_1.1_spmd, %region_2.6_spmd} | conditional | flops 1159219200 | bytes 29795432 | solution.py:96
  131.3 2.3 %bitcast_reduce_fusion = (f32[8,128]{1,0:T(8,128)S(1)}, f32[2048,128,8]{1,0,2:T(8,128)S(1)}) fusion(bf16[4,128,8,128]{3,1,2,0:T(8,128)(2,1)S(1)} %get-tuple-element.62, s32[]{:T(128)S(6)} %select_n.22, bf16[4,2048,1,128]{3,1,2,0:T(8,128)(2,1)} %get-tuple-element.61, s32[]{:T(128)S(6)} %select_n.23), kind=kOutput, calls=%fused_computation.1 | convolution fusion | flops 541064192 | bytes 9179144 | tf_op jit(solution)/shard_map/while/body/eval_jaxpr/cond/branch_1_fun/tkgd,skd->kgts/dot_general | solution.py:22
  138.8 2.5 %copy.18 = bf16[4,128,8,128]{3,2,1,0:T(8,128)(2,1)} copy(bf16[4,128,8,128]{1,3,2,0:T(8,128)(2,1)} %get-tuple-element.79) | data formatting | bytes 2097152 | tf_op jit(solution)/shard_map/while | solution.py:98
  141.5 18.2 %psum.7 = f32[1,4,128,2]{2,3,1,0:T(2,128)} all-reduce(f32[1,4,128,2]{2,3,1,0:T(2,128)S(1)} %convolution_bitcast_fusion.1), channel_id=1, replica_groups=mesh['dp'=64,'mp'=8] {'mp'}, use_global_device_ids=true, to_apply=%region_8.9 | all-reduce | flops 1024 | bytes 8192 | tf_op jit(solution)/shard_map/psum | solution.py:102
  (69 shorter events, 30.4 us)
Async XLA Ops:
  0.6 140.6 %copy-start = (bf16[8,128,2]{1,2,0:T(2,128)(2,1)S(1)}, bf16[8,128,2]{1,2,0:T(2,128)(2,1)}, u32[]{:S(2)}) copy-start(bf16[8,128,2]{1,2,0:T(2,128)(2,1)} %param.19) | copy-start | bytes 12292
  0.6 22.0 %copy-start.6 = (bf16[1,4,128,1,128]{4,2,3,1,0:T(8,128)(2,1)S(1)}, bf16[1,4,128,1,128]{4,2,3,1,0:T(8,128)(2,1)}, u32[]{:S(2)}) copy-start(bf16[1,4,128,1,128]{4,2,3,1,0:T(8,128)(2,1)} %param.14) | copy-start | bytes 393220
  0.7 22.1 %copy-start.7 = (s32[1,4]{1,0:T(1,128)S(1)}, s32[1,4]{1,0:T(1,128)}, u32[]{:S(2)}) copy-start(s32[1,4]{1,0:T(1,128)} %param.18) | copy-start | bytes 52
  2.0 20.8 %copy-start.2 = (bf16[1,2048,1,128]{1,3,2,0:T(8,128)(2,1)}, bf16[1,2048,1,128]{1,3,2,0:T(8,128)(2,1)S(1)}, u32[]{:S(2)}) copy-start(bf16[1,2048,1,128]{1,3,2,0:T(8,128)(2,1)S(1)} %copy.15) | copy-start | bytes 1572868
  2.0 13.5 %collective-permute-start = (bf16[1,2048,1,128]{1,3,2,0:T(8,128)(2,1)S(1)}, bf16[1,2048,1,128]{1,3,2,0:T(8,128)(2,1)S(1)}, u32[]{:S(2)}, u32[]{:S(2)}) collective-permute-start(bf16[1,2048,1,128]{1,3,2,0:T(8,128)(2,1)S(1)} %copy.15), channel_id=1, source_target_pairs={{0,8},{8,16},{16,24},{24,32},{32,40},{40,48},{48,56},{56,64},{64,7... | collective-permute-start | bytes 1572872 | tf_op jit(solution)/shard_map/ppermute | solution.py:15
  3.9 18.9 %collective-permute-start.1 = (bf16[1,2048,1,128]{1,3,2,0:T(8,128)(2,1)S(1)}, bf16[1,2048,1,128]{1,3,2,0:T(8,128)(2,1)S(1)}, u32[]{:S(2)}, u32[]{:S(2)}) collective-permute-start(bf16[1,2048,1,128]{1,3,2,0:T(8,128)(2,1)S(1)} %copy.15), channel_id=1, source_target_pairs={{0,16},{8,24},{16,32},{24,40},{32,48},{40,56},{48,64},{56,72},{64,... | collective-permute-start | bytes 1572872 | tf_op jit(solution)/shard_map/ppermute | solution.py:15
  5.8 37.9 %collective-permute-start.2 = (bf16[1,2048,1,128]{1,3,2,0:T(8,128)(2,1)S(1)}, bf16[1,2048,1,128]{1,3,2,0:T(8,128)(2,1)}, u32[]{:S(2)}, u32[]{:S(2)}) collective-permute-start(bf16[1,2048,1,128]{1,3,2,0:T(8,128)(2,1)S(1)} %copy.15), channel_id=1, source_target_pairs={{0,24},{8,32},{16,40},{24,48},{32,56},{40,64},{48,72},{56,80},{64,... | collective-permute-start | bytes 1572872 | tf_op jit(solution)/shard_map/ppermute | solution.py:15
  7.7 47.2 %collective-permute-start.3 = (bf16[1,2048,1,128]{3,1,2,0:T(8,128)(2,1)}, bf16[1,2048,1,128]{3,1,2,0:T(8,128)(2,1)}, u32[]{:S(2)}, u32[]{:S(2)}) collective-permute-start(bf16[1,2048,1,128]{3,1,2,0:T(8,128)(2,1)} %param.15), channel_id=1, source_target_pairs={{0,8},{8,16},{16,24},{24,32},{32,40},{40,48},{48,56},{56,64},{64,7... | collective-permute-start | bytes 1572872 | tf_op jit(solution)/shard_map/ppermute | solution.py:15
  9.7 45.3 %collective-permute-start.4 = (bf16[1,2048,1,128]{3,1,2,0:T(8,128)(2,1)}, bf16[1,2048,1,128]{3,1,2,0:T(8,128)(2,1)}, u32[]{:S(2)}, u32[]{:S(2)}) collective-permute-start(bf16[1,2048,1,128]{3,1,2,0:T(8,128)(2,1)} %param.15), channel_id=1, source_target_pairs={{0,16},{8,24},{16,32},{24,40},{32,48},{40,56},{48,64},{56,72},{64,... | collective-permute-start | bytes 1572872 | tf_op jit(solution)/shard_map/ppermute | solution.py:15
  15.5 0.8 copy-start.4
  16.3 58.0 %collective-permute-start.5 = (bf16[1,2048,1,128]{3,1,2,0:T(8,128)(2,1)}, bf16[1,2048,1,128]{3,1,2,0:T(8,128)(2,1)}, u32[]{:S(2)}, u32[]{:S(2)}) collective-permute-start(bf16[1,2048,1,128]{3,1,2,0:T(8,128)(2,1)} %param.15), channel_id=1, source_target_pairs={{0,24},{8,32},{16,40},{24,48},{32,56},{40,64},{48,72},{56,80},{64,... | collective-permute-start | bytes 1572872 | tf_op jit(solution)/shard_map/ppermute | solution.py:15
  22.8 51.6 %copy-start.3 = (bf16[1,2048,1,128]{3,1,2,0:T(8,128)(2,1)S(1)}, bf16[1,2048,1,128]{3,1,2,0:T(8,128)(2,1)}, u32[]{:S(2)}) copy-start(bf16[1,2048,1,128]{3,1,2,0:T(8,128)(2,1)} %param.15) | copy-start | bytes 1572868
  22.8 0.8 copy-start.5
  138.8 2.5 %copy-start.1 = (bf16[4,128,8,128]{1,3,2,0:T(8,128)(2,1)S(1)}, bf16[4,128,8,128]{1,3,2,0:T(8,128)(2,1)}, u32[]{:S(2)}) copy-start(bf16[4,128,8,128]{1,3,2,0:T(8,128)(2,1)} %get-tuple-element.79) | copy-start | bytes 3145732
where the time goes:
time: 161 us; the launch traced here: 160 us
  waiting for transfers between devices  50.5 us (31%)
  loops' own time  24.8 us (15%)
  matrix products  21 us (13%)
  blocking collectives  18.2 us (11%)
  local copies, waits for them, and re-layouts  16.9 us (10%)
  starting transfers between devices  16.1 us (10%)
  other arithmetic  10.7 us (7%)
    ppermute x6, waiting for transfers between devices, passed_along(): return lax.ppermute(value, axis, pairs)  50.5 us
    psum x1, blocking collectives, shards(): logits = lax.psum(partial_logits, 'mp')  18.2 us
    ppermute x6, starting transfers between devices, passed_along(): return lax.ppermute(value, axis, pairs)  16.1 us
    another operation x4, loops' own time, guarded(): return lax.cond(active[member], finish, vacant, member)  14.8 us
    dot_general x8, matrix products, attend_part(): jnp.einsum('tkgd,skd->kgts', grouped, key_rows, preferred_element_type=jn...  13.2 us
    another operation x1, loops' own time, shards(): attended = lax.map(guarded, slot_ids)  10.1 us
    dot_general x8, matrix products, attend_part(): jnp.einsum('kgts,skd->tkgd', weights.astype(jnp.bfloat16), value_rows, pr...  7.53 us
    reduce_sum x8, other arithmetic, attend_part(): row_total = jnp.sum(weights, axis=-1)  5.8 us
  transfers between devices with their start and end apart: 6, of which 4 were waited for; matrix products, arithmetic and copies ran while one was open for 2% of the time, Pallas kernels for 0%

commit v1 on v0

v1 whole, which is shorter than its diff:
```python
import functools

import jax
import jax.numpy as jnp
from jax import lax
from jax.experimental import pallas as pl
from jax.experimental.pallas import tpu as pltpu
from jax.sharding import PartitionSpec as P

MESH = pl.DeviceIdType.MESH
CHUNKS = 8
AHEAD = 2
COLS = 256
LOG2E = 1.4426950408889634
NEG = -1.0e30


def kernel(
    n_dp,
    n_mp,
    q_hbm,
    ck_hbm,
    cv_hbm,
    pk_hbm,
    pv_hbm,
    w_ref,
    count_ref,
    parent_ref,
    att_ref,
    logit_ref,
    *scratch,
):
    bufs = scratch[:CHUNKS]
    (q_ref, ck_ref, cv_ref, acc_ref, m_ref, l_ref, part_ref, gather_ref) = scratch[CHUNKS : CHUNKS + 8]
    (in_sem, own_sem, recv_sem, z_sem, d2d_sem, fwd_sem, y_send, y_recv) = scratch[CHUNKS + 8 :]
    slots, rows, size = q_ref.shape
    chunk = bufs[0].shape[2]
    heads = w_ref.shape[0] // 2
    scale = LOG2E * size**-0.5

    dp = lax.axis_index("dp")
    mp = lax.axis_index("mp")
    core = lax.rem(dp, 2)
    mate = dp + 1 - 2 * core
    ahead = lax.rem(dp + 2, n_dp)
    behind = lax.rem(dp + n_dp - 2, n_dp)
    cross = lax.rem(dp + n_dp + 2 * core - 1, n_dp)

    loads = [
        pltpu.make_async_copy(q_hbm, q_ref, in_sem.at[0]),
        pltpu.make_async_copy(ck_hbm, ck_ref, in_sem.at[1]),
        pltpu.make_async_copy(cv_hbm, cv_ref, in_sem.at[2]),
    ]
    for copy in loads:
        copy.start()

    def part(j):
        return pl.ds(j * chunk, chunk)

    sources = (pk_hbm, pv_hbm)

    def own(j, kind):
        return pltpu.make_async_copy(sources[kind].at[part(j)], bufs[j].at[0, kind], own_sem.at[j, kind])

    barrier = pltpu.get_barrier_semaphore()
    for other in (mate, ahead, behind, cross):
        pl.semaphore_signal(barrier, inc=1, device_id=(other, mp), device_id_type=MESH)
    for step in range(1, n_mp):
        pl.semaphore_signal(barrier, inc=1, device_id=(dp, lax.rem(mp + step, n_mp)), device_id_type=MESH)
    for j in range(CHUNKS):
        for kind in (0, 1):
            own(j, kind).start()
    pl.semaphore_wait(barrier, 4 + n_mp - 1)

    def remote(src, j, slot, kind, sem, target):
        return pltpu.make_async_remote_copy(
            src_ref=src,
            dst_ref=bufs[j].at[slot, kind],
            send_sem=sem,
            recv_sem=recv_sem.at[slot - 1, j, kind],
            device_id=(target, mp),
            device_id_type=MESH,
        )

    def z_send(j, kind):
        return remote(sources[kind].at[part(j)], j, 2, kind, z_sem.at[j, kind], ahead)

    def own_to_mate(j, kind):
        return remote(sources[kind].at[part(j)], j, 1, kind, d2d_sem.at[j, kind], mate)

    def two_to_mate(j, kind, slot):
        return remote(bufs[j].at[2, kind], j, slot, kind, fwd_sem.at[j, kind], mate)

    def two_to_next(j, kind):
        return remote(bufs[j].at[2, kind], j, 3, kind, d2d_sem.at[j, kind], cross)

    def wait_slot(j, slot):
        for kind in (0, 1):
            remote(bufs[j].at[slot, kind], j, slot, kind, z_sem.at[j, kind], mate).wait_recv()

    def start_z(j):
        for kind in (0, 1):
            z_send(j, kind).start()

        @pl.when(core == 0)
        def _():
            for kind in (0, 1):
                own_to_mate(j, kind).start()

    def forward(j):
        @pl.when(core == 0)
        def _():
            for kind in (0, 1):
                two_to_mate(j, kind, 3).start()

        @pl.when(core == 1)
        def _():
            for kind in (0, 1):
                two_to_next(j, kind).start()
            for kind in (0, 1):
                two_to_mate(j, kind, 1).start()

    for j in range(AHEAD):
        start_z(j)

    for copy in loads:
        copy.wait()

    def first(c, _):
        keys = ck_ref[c]
        values = cv_ref[c].T
        for start in range(0, rows, COLS):
            cols = pl.ds(start, COLS)
            s = lax.dot_general(keys, q_ref[c, cols], (((1,), (1,)), ((), ())), preferred_element_type=jnp.float32)
            key_at = lax.broadcasted_iota(jnp.int32, s.shape, 0)
            row_at = (lax.broadcasted_iota(jnp.int32, s.shape, 1) + start) // heads
            s = jnp.where(key_at <= row_at, s, NEG)
            peak = jnp.max(s, axis=0, keepdims=True)
            p = jnp.exp2((s - peak) * scale)
            m_ref[c, :, cols] = peak
            l_ref[c, :, cols] = jnp.sum(p, axis=0, keepdims=True)
            acc_ref[c, :, cols] = jnp.dot(values, p.astype(jnp.bfloat16), preferred_element_type=jnp.float32)
        return 0

    lax.fori_loop(0, slots, first, 0)

    def compute(j):
        for kind in (0, 1):
            own(j, kind).wait()
        wait_slot(j, 1)
        wait_slot(j, 3)

        def one(c, _):
            distance = jnp.bitwise_and(dp - parent_ref[0, c], 3)
            keys = bufs[j][distance, 0]
            values = bufs[j][distance, 1].T
            for start in range(0, rows, COLS):
                cols = pl.ds(start, COLS)
                s = lax.dot_general(keys, q_ref[c, cols], (((1,), (1,)), ((), ())), preferred_element_type=jnp.float32)
                old = m_ref[c, :, cols]
                peak = jnp.maximum(old, jnp.max(s, axis=0, keepdims=True))
                p = jnp.exp2((s - peak) * scale)
                alpha = jnp.exp2((old - peak) * scale)
                m_ref[c, :, cols] = peak
                l_ref[c, :, cols] = l_ref[c, :, cols] * alpha + jnp.sum(p, axis=0, keepdims=True)
                acc_ref[c, :, cols] = acc_ref[c, :, cols] * alpha + jnp.dot(
                    values, p.astype(jnp.bfloat16), preferred_element_type=jnp.float32
                )
            return 0

        lax.fori_loop(0, slots, one, 0)

    for j in range(CHUNKS):
        wait_slot(j, 2)
        forward(j)
        if j + AHEAD < CHUNKS:
            start_z(j + AHEAD)
        if j >= 1:
            compute(j - 1)
    compute(CHUNKS - 1)

    weight = w_ref[...]
    head_at = lax.broadcasted_iota(jnp.int32, (rows, 2 * heads), 0) % heads
    weight_at = lax.broadcasted_iota(jnp.int32, (rows, 2 * heads), 1) // 2
    same = head_at == weight_at
    pick = (
        lax.broadcasted_iota(jnp.int32, (2, 2 * heads), 0) == lax.broadcasted_iota(jnp.int32, (2, 2 * heads), 1) % 2
    ).astype(jnp.float32)

    def last(c, _):
        live = c < count_ref[0]
        done = acc_ref[c] * (1.0 / l_ref[c])
        done = jnp.where(live, done, 0.0).astype(jnp.bfloat16).T
        att_ref[c] = done
        z = lax.dot_general(done, weight, (((1,), (1,)), ((), ())), preferred_element_type=jnp.float32)
        z = jnp.where(same, z, 0.0).reshape(rows // heads, heads, 2 * heads)
        z = jnp.sum(z, axis=1)
        part_ref[c] = lax.dot_general(
            pick, z, (((1,), (1,)), ((), ())), preferred_element_type=jnp.float32, precision=lax.Precision.HIGHEST
        )
        return 0

    lax.fori_loop(0, slots, last, 0)

    def to_peer(step):
        return pltpu.make_async_remote_copy(
            src_ref=part_ref,
            dst_ref=gather_ref.at[step - 1],
            send_sem=y_send.at[step - 1],
            recv_sem=y_recv.at[step - 1],
            device_id=(dp, lax.rem(mp + step, n_mp)),
            device_id_type=MESH,
        )

    for step in range(1, n_mp):
        to_peer(step).start()
    total = part_ref[...]
    for step in range(1, n_mp):
        to_peer(step).wait_recv()
        total = total + gather_ref[step - 1]
    logit_ref[...] = total

    for step in range(1, n_mp):
        to_peer(step).wait_send()
    for j in range(CHUNKS):
        for kind in (0, 1):
            z_send(j, kind).wait_send()
            own_to_mate(j, kind).wait_send()
            two_to_mate(j, kind, 3).wait_send()


def solution(mesh):
    n_dp, n_mp = mesh.shape["dp"], mesh.shape["mp"]

    def step(queries, keys, values, prefix_keys, prefix_values, count, parent, weight):
        _, slots, steps, heads, size = queries.shape
        prefix = prefix_keys.shape[1]
        rows = steps * heads
        chunk = prefix // CHUNKS
        hbm = pl.BlockSpec(memory_space=pl.ANY)
        vmem = pl.BlockSpec(memory_space=pltpu.VMEM)
        smem = pl.BlockSpec(memory_space=pltpu.SMEM)
        bf16, f32 = jnp.bfloat16, jnp.float32
        attended, logits = pl.pallas_call(
            functools.partial(kernel, n_dp, n_mp),
            out_shape=(
                jax.ShapeDtypeStruct((slots, rows, size), bf16),
                jax.ShapeDtypeStruct((slots, 2, steps), f32),
            ),
            in_specs=[hbm, hbm, hbm, hbm, hbm, vmem, smem, smem],
            out_specs=(vmem, vmem),
            scratch_shapes=[pltpu.VMEM((4, 2, chunk, size), bf16)] * CHUNKS
            + [
                pltpu.VMEM((slots, rows, size), bf16),
                pltpu.VMEM((slots, steps, size), bf16),
                pltpu.VMEM((slots, steps, size), bf16),
                pltpu.VMEM((slots, size, rows), f32),
                pltpu.VMEM((slots, 1, rows), f32),
                pltpu.VMEM((slots, 1, rows), f32),
                pltpu.VMEM((slots, 2, steps), f32),
                pltpu.VMEM((n_mp - 1, slots, 2, steps), f32),
                pltpu.SemaphoreType.DMA((3,)),
                pltpu.SemaphoreType.DMA((CHUNKS, 2)),
                pltpu.SemaphoreType.DMA((3, CHUNKS, 2)),
                pltpu.SemaphoreType.DMA((CHUNKS, 2)),
                pltpu.SemaphoreType.DMA((CHUNKS, 2)),
                pltpu.SemaphoreType.DMA((CHUNKS, 2)),
                pltpu.SemaphoreType.DMA((n_mp - 1,)),
                pltpu.SemaphoreType.DMA((n_mp - 1,)),
            ],
            compiler_params=pltpu.CompilerParams(
                collective_id=0, has_side_effects=True, vmem_limit_bytes=48 * 1024 * 1024
            ),
            name="prefix_attention",
        )(
            queries.reshape(slots, rows, size),
            keys.reshape(slots, steps, size),
            values.reshape(slots, steps, size),
            prefix_keys.reshape(prefix, size),
            prefix_values.reshape(prefix, size),
            jnp.transpose(weight, (0, 2, 1)).reshape(2 * heads, size),
            count,
            parent,
        )
        attended = attended.reshape(1, slots, steps, heads, size)
        return attended, jnp.transpose(logits, (0, 2, 1))[None]

    return jax.shard_map(
        step,
        mesh=mesh,
        in_specs=(
            P("dp", None, None, "mp", None),
            P("dp", None, None, "mp", None),
            P("dp", None, None, "mp", None),
            P("dp", None, "mp", None),
            P("dp", None, "mp", None),
            P("dp"),
            P("dp", None),
            P("mp", None, None),
        ),
        out_specs=(P("dp", None, None, "mp", None), P("dp", None, None, None)),
        check_vma=False,
    )
```

time: 161 us -> 82.8 us (0.51)
  the two profiles are of different devices: /device:TPU:448 before, /device:TPU:1 now
where the time goes in v1:
time: 82.8 us; the launch traced here: 81.4 us
  Pallas kernels  72.7 us (88%)
  local copies, waits for them, and re-layouts  7.35 us (9%)
  between operations  1.31 us (2%)
    pallas_call x1, Pallas kernels, step(): pl.pallas_call(functools.partial(kernel, n_dp, n_mp), out_shape=(jax.Shap...  72.7 us
    unnamed x16, local copies, waits for them, and re-layouts  7.35 us

profile of v1, /device:TPU:1, one launch (start us, length us, event | category | flops | bytes accessed | tf_op | source)
XLA Modules:
  0.0 81.4 jit_solution(18097194054821026492)
XLA Ops:
  1.3 0.0 copy-start.5
  1.3 0.0 copy-start.6
  1.3 0.7 copy-done.5
  2.0 0.0 copy-done.6
  2.0 0.0 copy-start
  2.0 1.2 %copy-done = bf16[1,4,128,8,128]{4,3,2,1,0:T(8,128)(2,1)S(1)} copy-done((bf16[1,4,128,8,128]{4,3,2,1,0:T(8,128)(2,1)S(1)}, bf16[1,4,128,8,128]{4,3,2,1,0:T(8,128)(2,1)}, u32[]{:S(2)}) %copy-start) | copy-done | bytes 1048600
  3.2 0.0 copy-start.1
  3.2 1.0 %copy-done.1 = bf16[1,2048,1,128]{3,1,2,0:T(8,128)(2,1)S(1)} copy-done((bf16[1,2048,1,128]{3,1,2,0:T(8,128)(2,1)S(1)}, bf16[1,2048,1,128]{3,1,2,0:T(8,128)(2,1)}, u32[]{:S(2)}) %copy-start.1) | copy-done | bytes 524312
  4.2 0.0 copy-start.2
  4.2 1.0 %copy-done.2 = bf16[1,2048,1,128]{3,1,2,0:T(8,128)(2,1)S(1)} copy-done((bf16[1,2048,1,128]{3,1,2,0:T(8,128)(2,1)S(1)}, bf16[1,2048,1,128]{3,1,2,0:T(8,128)(2,1)}, u32[]{:S(2)}) %copy-start.2) | copy-done | bytes 524312
  5.3 0.0 copy-start.3
  5.3 0.9 %copy-done.3 = bf16[1,4,128,1,128]{4,2,3,1,0:T(8,128)(2,1)S(1)} copy-done((bf16[1,4,128,1,128]{4,2,3,1,0:T(8,128)(2,1)S(1)}, bf16[1,4,128,1,128]{4,2,3,1,0:T(8,128)(2,1)}, u32[]{:S(2)}) %copy-start.3) | copy-done | bytes 131096
  6.2 0.0 copy-start.4
  6.2 0.9 %copy-done.4 = bf16[1,4,128,1,128]{4,2,3,1,0:T(8,128)(2,1)S(1)} copy-done((bf16[1,4,128,1,128]{4,2,3,1,0:T(8,128)(2,1)S(1)}, bf16[1,4,128,1,128]{4,2,3,1,0:T(8,128)(2,1)}, u32[]{:S(2)}) %copy-start.4) | copy-done | bytes 131096
  7.1 72.7 %prefix_attention.1 = (bf16[4,1024,128]{2,1,0:T(8,128)(2,1)S(1)}, f32[4,2,128]{2,1,0:T(2,128)S(1)}) custom-call(bf16[4,1024,128]{2,1,0:T(8,128)(2,1)S(1)} %bitcast.12, bf16[4,128,128]{2,1,0:T(8,128)(2,1)S(1)} %bitcast.16, bf16[4,128,128]{2,1,0:T(8,128)(2,1)S(1)} %bitcast.17, bf16[2048,128]{1,0:T(8,128)(2,1)S(1)} %bitcast.14, bf16[2048,128]{1,0:T(8,128)(2,1)S(1)} %bitcast.15, ...), custom_call_target="tpu_custom_call" | custom-call | tf_op jit(solution)/shard_map/prefix_attention/pallas_call | solution.py:244
  79.8 1.0 %copy.13 = bf16[1,4,128,8,128]{4,3,2,1,0:T(8,128)(2,1)} copy(bf16[1,4,128,8,128]{4,3,2,1,0:T(8,128)(2,1)S(1)} %bitcast.13) | data formatting | bytes 2097152
  80.8 0.6 copy.14
Async XLA Ops:
  1.3 0.7 copy-start.5
  1.3 0.7 copy-start.6
  2.0 1.2 %copy-start = (bf16[1,4,128,8,128]{4,3,2,1,0:T(8,128)(2,1)S(1)}, bf16[1,4,128,8,128]{4,3,2,1,0:T(8,128)(2,1)}, u32[]{:S(2)}) copy-start(bf16[1,4,128,8,128]{4,3,2,1,0:T(8,128)(2,1)} %param.8) | copy-start | bytes 3145732
  3.2 1.0 %copy-start.1 = (bf16[1,2048,1,128]{3,1,2,0:T(8,128)(2,1)S(1)}, bf16[1,2048,1,128]{3,1,2,0:T(8,128)(2,1)}, u32[]{:S(2)}) copy-start(bf16[1,2048,1,128]{3,1,2,0:T(8,128)(2,1)} %param.11) | copy-start | bytes 1572868
  4.2 1.0 %copy-start.2 = (bf16[1,2048,1,128]{3,1,2,0:T(8,128)(2,1)S(1)}, bf16[1,2048,1,128]{3,1,2,0:T(8,128)(2,1)}, u32[]{:S(2)}) copy-start(bf16[1,2048,1,128]{3,1,2,0:T(8,128)(2,1)} %param.12) | copy-start | bytes 1572868
  5.3 0.9 %copy-start.3 = (bf16[1,4,128,1,128]{4,2,3,1,0:T(8,128)(2,1)S(1)}, bf16[1,4,128,1,128]{4,2,3,1,0:T(8,128)(2,1)}, u32[]{:S(2)}) copy-start(bf16[1,4,128,1,128]{4,2,3,1,0:T(8,128)(2,1)} %param.9) | copy-start | bytes 393220
  6.2 0.9 %copy-start.4 = (bf16[1,4,128,1,128]{4,2,3,1,0:T(8,128)(2,1)S(1)}, bf16[1,4,128,1,128]{4,2,3,1,0:T(8,128)(2,1)}, u32[]{:S(2)}) copy-start(bf16[1,4,128,1,128]{4,2,3,1,0:T(8,128)(2,1)} %param.10) | copy-start | bytes 393220

commit v2 on v1

v2 whole, which is shorter than its diff:
```python
import functools

import jax
import jax.numpy as jnp
from jax import lax
from jax.experimental import pallas as pl
from jax.experimental.pallas import tpu as pltpu
from jax.sharding import PartitionSpec as P

MESH = pl.DeviceIdType.MESH
SIZES = (8, 8, 8, 8, 8, 8, 8, 8)
DETOUR = ()
RELAY = ((0, 1, 2), (3, 4, 5), (6, 7), (), (), (), (), ())
AHEAD = 4
COLS = 256
EXTRA = 16
RING = 8
LOG2E = 1.4426950408889634
NEG = -1.0e30
VMEM_LIMIT = 60 * 1024 * 1024


def kernel(n_dp, n_mp, q_hbm, ck_hbm, cv_hbm, pk_hbm, pv_hbm, w_hbm, count_hbm, parent_hbm, att_ref, logit_ref, *scratch):
    scratch = list(scratch)

    def take(n):
        taken, scratch[:n] = scratch[:n], []
        return taken

    chunks = len(SIZES)
    bufs, relays = take(chunks), take(chunks)
    q_ref, ck_ref, cv_ref, w_ref, count_ref, parent_ref = take(6)
    acc_ref, m_ref, qq_ref, part_ref, gather_ref, z_ref, vt_ref, member_ref, done_ref = take(9)
    s_ref, top_ref, p_ref, alpha_ref = take(4)
    in_sem, own_sem, recv_sem, z_sem, d2d_sem, fwd_sem, out_sem, relay_sem, pass_sem, y_send, y_recv = scratch

    slots, rows, size = q_ref.shape
    prefix = pk_hbm.shape[0]
    heads = w_ref.shape[0] // 2
    blocks = rows // COLS
    scale = LOG2E * size**-0.5
    sizes = [prefix * n // sum(SIZES) for n in SIZES]
    most = max(sizes)
    starts = [sum(sizes[:j]) for j in range(chunks)]

    dp = lax.axis_index("dp")
    mp = lax.axis_index("mp")
    core = lax.rem(dp, 2)
    z = lax.rem(dp // 2, RING)
    plane = dp // (2 * RING)
    planes = n_dp // (2 * RING)

    def at(x, chip, which):
        return (lax.rem(x + planes, planes) * RING + chip) * 2 + which

    mate = dp + 1 - 2 * core
    ahead = lax.rem(dp + 2, n_dp)
    behind = lax.rem(dp + n_dp - 2, n_dp)
    cross = lax.rem(dp + n_dp + 2 * core - 1, n_dp)
    via = at(plane + (z + 2) // RING, lax.rem(z + RING - 3, RING), 1)
    served = lax.rem(z + 3, RING)
    served_from = at(plane - (served + 2) // RING, served, 1)
    drop = at(plane, lax.rem(served + 2, RING), 0)
    brought = at(plane, lax.rem(z + 3, RING), 1)

    sources = (pk_hbm, pv_hbm)

    def part(j):
        return pl.ds(starts[j], sizes[j])

    def own(j, kind):
        return pltpu.make_async_copy(sources[kind].at[part(j)], bufs[j].at[0, kind], own_sem.at[j])

    def own_whole(j):
        return pltpu.make_async_copy(bufs[j].at[1], bufs[j].at[0], own_sem.at[j])

    loads = [
        pltpu.make_async_copy(src, dst, in_sem.at[k])
        for k, (src, dst) in enumerate(
            (
                (parent_hbm, parent_ref),
                (count_hbm, count_ref),
                (q_hbm, q_ref),
                (ck_hbm, ck_ref),
                (cv_hbm, cv_ref),
                (w_hbm, w_ref),
            )
        )
    ]

    barrier = pltpu.get_barrier_semaphore()

    def greet(*others):
        for other in others:
            pl.semaphore_signal(barrier, inc=1, device_id=(other, mp), device_id_type=MESH)

    greet(mate, ahead, behind, cross)
    for step in range(1, n_mp):
        pl.semaphore_signal(barrier, inc=1, device_id=(dp, lax.rem(mp + step, n_mp)), device_id_type=MESH)

    @pl.when(core == 0)
    def _():
        greet(brought)

    @pl.when(core == 1)
    def _():
        greet(via, served_from, drop)

    for copy in loads:
        copy.start()
    for j in range(chunks):
        for kind in (0, 1):
            own(j, kind).start()
    pl.semaphore_wait(barrier, 4 + n_mp - 1 + 1 + 2 * core)

    def remote(src, dst, send, recv, target):
        return pltpu.make_async_remote_copy(
            src_ref=src, dst_ref=dst, send_sem=send, recv_sem=recv, device_id=(target, mp), device_id_type=MESH
        )

    def to_ahead(j, kind):
        return remote(sources[kind].at[part(j)], bufs[j].at[2, kind], z_sem.at[j], recv_sem.at[1, j], ahead)

    def own_to_mate(j, kind):
        return remote(sources[kind].at[part(j)], bufs[j].at[1, kind], d2d_sem.at[j], recv_sem.at[0, j], mate)

    def own_to_via(j, kind):
        return remote(sources[kind].at[part(j)], relays[j].at[kind], out_sem.at[j], relay_sem.at[j], via)

    def two_to_mate(j, slot):
        return remote(bufs[j].at[2], bufs[j].at[slot], fwd_sem.at[j], recv_sem.at[slot - 1, j], mate)

    def two_to_next(j):
        return remote(bufs[j].at[2], bufs[j].at[3], d2d_sem.at[j], recv_sem.at[2, j], cross)

    def relay_on(j):
        return remote(relays[j], bufs[j].at[3], pass_sem.at[j], recv_sem.at[2, j], drop)

    def whole(j, send, recv):
        return remote(bufs[j].at[2], bufs[j].at[1], send, recv, mate)

    def wait_slot(j, slot):
        whole(j, z_sem.at[j], recv_sem.at[slot - 1, j]).wait_recv()

    def wait_sent(j, sem):
        whole(j, sem.at[j], recv_sem.at[0, j]).wait_send()

    def on_ring(j, owner, do):
        if j in DETOUR:
            do()
        else:
            pl.when(lax.rem(owner + 2, RING) == 0)(do)

    def off_ring(j, owner, do):
        if j not in DETOUR:
            pl.when(lax.rem(owner + 2, RING) != 0)(do)

    def start_direct(j):
        for kind in (0, 1):
            to_ahead(j, kind).start()

        @pl.when(core == 0)
        def _():
            for kind in (0, 1):
                own_to_mate(j, kind).start()

    def start_detour(j):
        def do():
            for kind in (0, 1):
                own_to_via(j, kind).start()

        on_ring(j, z, do)

    def pass_on(j):
        def do():
            remote(relays[j], relays[j], out_sem.at[j], relay_sem.at[j], via).wait_recv()
            relay_on(j).start()

        on_ring(j, served, do)

    def forward(j):
        @pl.when(core == 0)
        def _():
            two_to_mate(j, 3).start()

        @pl.when(core == 1)
        def _():
            two_to_mate(j, 1).start()
            off_ring(j, lax.rem(z + RING - 1, RING), lambda: two_to_next(j).start())

    def settle(j):
        wait_sent(j, z_sem)
        wait_sent(j, fwd_sem)

        @pl.when(core == 0)
        def _():
            wait_sent(j, d2d_sem)

        @pl.when(core == 1)
        def _():
            off_ring(j, lax.rem(z + RING - 1, RING), lambda: wait_sent(j, d2d_sem))
            on_ring(j, z, lambda: wait_sent(j, out_sem))
            on_ring(j, served, lambda: wait_sent(j, pass_sem))

    start_direct(0)

    @pl.when(core == 1)
    def _():
        for j in range(chunks):
            start_detour(j)

    for j in range(1, AHEAD):
        start_direct(j)
    eager = lax.rem(z + 1, RING) <= 1

    @pl.when(eager)
    def _():
        for j in range(AHEAD, chunks):
            start_direct(j)

    for copy in loads:
        copy.wait()

    def cols_of(b):
        return pl.ds(b * COLS, COLS)

    def scaled(c, _):
        for b in range(blocks):
            wide = q_ref[c, cols_of(b)].astype(jnp.float32) * scale
            high = wide.astype(jnp.bfloat16)
            qq_ref[c, cols_of(b), :size] = high
            qq_ref[c, cols_of(b), size:] = (wide - high.astype(jnp.float32)).astype(jnp.bfloat16)
        return 0

    lax.fori_loop(0, slots, scaled, 0)

    def score(c, b, keys, causal):
        n = keys.shape[0]
        s = lax.dot_general(
            jnp.concatenate([keys, keys], axis=1),
            qq_ref[c, cols_of(b)],
            (((1,), (1,)), ((), ())),
            preferred_element_type=jnp.float32,
        )
        if causal:
            key_at = lax.broadcasted_iota(jnp.int32, s.shape, 0)
            row_at = (lax.broadcasted_iota(jnp.int32, s.shape, 1) + b * COLS) // heads
            s = jnp.where(key_at <= row_at, s, NEG)
        s_ref[:n, cols_of(b)] = s
        top_ref[:, cols_of(b)] = jnp.max(s.reshape(n // 8, 8, COLS), axis=0)

    def weigh(c, b, n):
        cols = cols_of(b)
        old = m_ref[c, :, cols]
        peak = jnp.maximum(old, jnp.max(top_ref[:, cols], axis=0, keepdims=True))
        m_ref[c, :, cols] = peak
        alpha_ref[:, cols] = jnp.exp2(old - peak)
        p_ref[:n, cols] = jnp.exp2(s_ref[:n, cols] - peak).astype(jnp.bfloat16)

    def gather(c, b, values):
        cols = cols_of(b)
        acc_ref[c, :, cols] = acc_ref[c, :, cols] * alpha_ref[:, cols] + jnp.dot(
            values, p_ref[:, cols], preferred_element_type=jnp.float32
        )

    def keep_columns(values):
        n = values.shape[0]
        vt_ref[:size, :n] = values.T
        if n < most:
            vt_ref[:size, n:] = jnp.zeros((size, most - n), jnp.bfloat16)
        vt_ref[size:, :] = (lax.broadcasted_iota(jnp.int32, (EXTRA, most), 1) < n).astype(jnp.bfloat16)

    def stages(c, n, values, scored, keys, causal):
        earlier = vt_ref[...]
        for b in range(blocks):
            gather(jnp.bitwise_and(c + slots - 1, slots - 1), b, earlier)
            weigh(c, b, n)
            if keys is not None:
                score(scored, b, keys, causal)
        keep_columns(values)

    def zero(c, _):
        acc_ref[c] = jnp.zeros(acc_ref.shape[1:], jnp.float32)
        m_ref[c] = jnp.full(m_ref.shape[1:], NEG, jnp.float32)
        return 0

    lax.fori_loop(0, slots, zero, 0)
    vt_ref[...] = jnp.zeros(vt_ref.shape, jnp.bfloat16)
    p_ref[...] = jnp.zeros(p_ref.shape, jnp.bfloat16)
    alpha_ref[...] = jnp.ones(alpha_ref.shape, jnp.float32)

    group = lax.broadcasted_iota(jnp.int32, member_ref.shape, 0) // heads
    member_ref[...] = (group == lax.broadcasted_iota(jnp.int32, member_ref.shape, 1)).astype(jnp.bfloat16)
    to_row = lax.broadcasted_iota(jnp.int32, (2 * heads, 2 * heads), 0)
    from_row = lax.broadcasted_iota(jnp.int32, (2 * heads, 2 * heads), 1)
    order = (from_row == lax.rem(to_row, heads) * 2 + to_row // heads).astype(jnp.bfloat16)
    w_ref[...] = jnp.dot(order, w_ref[...], preferred_element_type=jnp.float32).astype(jnp.bfloat16)

    for b in range(blocks):
        score(0, b, ck_ref[0], True)

    def own_step(c, _):
        stages(c, ck_ref.shape[1], cv_ref[c], c + 1, ck_ref[c + 1], True)
        return 0

    lax.fori_loop(0, slots - 1, own_step, 0)

    def distance(c):
        return jnp.bitwise_and(dp - parent_ref[0, c], 3)

    def arrive(j):
        own_whole(j).wait()
        wait_slot(j, 1)
        wait_slot(j, 3)

    def cross_over(j):
        end = slots - 1
        values = cv_ref[end] if j == 0 else bufs[j - 1][distance(end), 1]
        keys = None if j == chunks else bufs[j][distance(0), 0]
        stages(end, values.shape[0], values, 0, keys, False)

    def compute(j):
        arrive(j)
        cross_over(j)

        def one(c, _):
            stages(c, sizes[j], bufs[j][distance(c), 1], c + 1, bufs[j][distance(c + 1), 0], False)
            return 0

        lax.fori_loop(0, slots - 1, one, 0)

    for j in range(chunks):
        wait_slot(j, 2)
        forward(j)
        if j + AHEAD < chunks:
            pl.when(jnp.logical_not(eager))(functools.partial(start_direct, j + AHEAD))

        @pl.when(core == 1)
        def _():
            for k in RELAY[j]:
                pass_on(k)

        if j >= 2:
            settle(j - 2)
        if j >= 1:
            compute(j - 1)
    compute(chunks - 1)
    cross_over(chunks)
    for b in range(blocks):
        gather(slots - 1, b, vt_ref[...])

    weight = w_ref[...]
    head_at = lax.broadcasted_iota(jnp.int32, (heads, rows), 1) % heads
    same = head_at == lax.broadcasted_iota(jnp.int32, (heads, rows), 0)

    def last(c, _):
        inverse = jnp.where(c < count_ref[0], 1.0 / acc_ref[c, size : size + 1], 0.0)
        done = (acc_ref[c, :size] * inverse).astype(jnp.bfloat16)
        done_ref[c] = done
        both = jnp.dot(weight, done, preferred_element_type=jnp.float32)
        for k in (0, 1):
            z_ref[c, k] = jnp.sum(jnp.where(same, both[k * heads : (k + 1) * heads], 0.0), axis=0, keepdims=True)
        return 0

    lax.fori_loop(0, slots, last, 0)

    lanes = z_ref[...].reshape(2 * slots, rows)
    high = lanes.astype(jnp.bfloat16)
    rest = lanes - high.astype(jnp.float32)
    middle = rest.astype(jnp.bfloat16)
    low = (rest - middle.astype(jnp.float32)).astype(jnp.bfloat16)
    sums = jnp.dot(jnp.concatenate([high, middle, low], axis=0), member_ref[...], preferred_element_type=jnp.float32)
    part_ref[...] = sums[: 2 * slots] + sums[2 * slots : 4 * slots] + sums[4 * slots :]

    def to_peer(step):
        return pltpu.make_async_remote_copy(
            src_ref=part_ref,
            dst_ref=gather_ref.at[step - 1],
            send_sem=y_send.at[step - 1],
            recv_sem=y_recv.at[step - 1],
            device_id=(dp, lax.rem(mp + step, n_mp)),
            device_id_type=MESH,
        )

    for step in range(1, n_mp):
        to_peer(step).start()

    def store(c, _):
        att_ref[c] = done_ref[c].T
        return 0

    lax.fori_loop(0, slots, store, 0)
    for j in range(max(chunks - 2, 0), chunks):
        settle(j)
    total = part_ref[...]
    for step in range(1, n_mp):
        to_peer(step).wait_recv()
        total = total + gather_ref[step - 1]
    logit_ref[...] = total
    for step in range(1, n_mp):
        to_peer(step).wait_send()


def solution(mesh):
    n_dp, n_mp = mesh.shape["dp"], mesh.shape["mp"]

    def step(queries, keys, values, prefix_keys, prefix_values, count, parent, weight):
        _, slots, steps, heads, size = queries.shape
        prefix = prefix_keys.shape[1]
        rows = steps * heads
        sizes = [prefix * n // sum(SIZES) for n in SIZES]
        chunks, most = len(sizes), max(sizes)
        bf16, f32 = jnp.bfloat16, jnp.float32
        dma = pltpu.SemaphoreType.DMA
        attended, logits = pl.pallas_call(
            functools.partial(kernel, n_dp, n_mp),
            out_shape=(
                jax.ShapeDtypeStruct((slots, rows, size), bf16),
                jax.ShapeDtypeStruct((2 * slots, steps), f32),
            ),
            in_specs=[pl.BlockSpec(memory_space=pltpu.HBM)] * 8,
            out_specs=(pl.BlockSpec(memory_space=pltpu.VMEM),) * 2,
            scratch_shapes=[pltpu.VMEM((4, 2, n, size), bf16) for n in sizes]
            + [pltpu.VMEM((2, n, size), bf16) for n in sizes]
            + [
                pltpu.VMEM((slots, rows, size), bf16),
                pltpu.VMEM((slots, steps, size), bf16),
                pltpu.VMEM((slots, steps, size), bf16),
                pltpu.VMEM((2 * heads, size), bf16),
                pltpu.SMEM((1,), jnp.int32),
                pltpu.SMEM((1, slots), jnp.int32),
                pltpu.VMEM((slots, size + EXTRA, rows), f32),
                pltpu.VMEM((slots, 1, rows), f32),
                pltpu.VMEM((slots, rows, 2 * size), bf16),
                pltpu.VMEM((2 * slots, steps), f32),
                pltpu.VMEM((max(n_mp - 1, 1), 2 * slots, steps), f32),
                pltpu.VMEM((slots, 2, 1, rows), f32),
                pltpu.VMEM((size + EXTRA, most), bf16),
                pltpu.VMEM((rows, steps), bf16),
                pltpu.VMEM((slots, size, rows), bf16),
            ]
            + [
                pltpu.VMEM((most, rows), f32),
                pltpu.VMEM((8, rows), f32),
                pltpu.VMEM((most, rows), bf16),
                pltpu.VMEM((1, rows), f32),
            ]
            + [dma((6,)), dma((chunks,)), dma((3, chunks))]
            + [dma((chunks,))] * 6
            + [dma((max(n_mp - 1, 1),))] * 2,
            compiler_params=pltpu.CompilerParams(
                collective_id=0, has_side_effects=True, vmem_limit_bytes=VMEM_LIMIT
            ),
            name="prefix_attention",
        )(
            queries.reshape(slots, rows, size),
            keys.reshape(slots, steps, size),
            values.reshape(slots, steps, size),
            prefix_keys.reshape(prefix, size),
            prefix_values.reshape(prefix, size),
            jnp.transpose(weight, (0, 2, 1)).reshape(2 * heads, size),
            count,
            parent,
        )
        attended = attended.reshape(1, slots, steps, heads, size)
        return attended, jnp.transpose(logits.reshape(slots, 2, steps), (0, 2, 1))[None]

    return jax.shard_map(
        step,
        mesh=mesh,
        in_specs=(
            P("dp", None, None, "mp", None),
            P("dp", None, None, "mp", None),
            P("dp", None, None, "mp", None),
            P("dp", None, "mp", None),
            P("dp", None, "mp", None),
            P("dp"),
            P("dp", None),
            P("mp", None, None),
        ),
        out_specs=(P("dp", None, None, "mp", None), P("dp", None, None, None)),
        check_vma=False,
    )
```

time: 82.8 us -> 66 us (0.80)
  the two profiles are of different devices: /device:TPU:1 before, /device:TPU:128 now
where the time goes in v2:
time: 66 us; the launch traced here: 65.9 us
  Pallas kernels  61.7 us (93%)
  local copies, waits for them, and re-layouts  2.86 us (4%)
  between operations  1.29 us (2%)
    pallas_call x1, Pallas kernels, step(): pl.pallas_call(functools.partial(kernel, n_dp, n_mp), out_shape=(jax.Shap...  61.7 us
    unnamed x4, local copies, waits for them, and re-layouts  2.86 us

profile of v2, /device:TPU:128, one launch (start us, length us, event | category | flops | bytes accessed | tf_op | source)
XLA Modules:
  0.0 65.9 jit_solution(12107119280830456032)
XLA Ops:
  1.3 61.7 %prefix_attention.1 = (bf16[4,1024,128]{2,1,0:T(8,128)(2,1)}, f32[8,128]{1,0:T(8,128)}) custom-call(bf16[4,1024,128]{2,1,0:T(8,128)(2,1)} %bitcast.14, bf16[4,128,128]{2,1,0:T(8,128)(2,1)} %bitcast.18, bf16[4,128,128]{2,1,0:T(8,128)(2,1)} %bitcast.19, bf16[2048,128]{1,0:T(8,128)(2,1)} %bitcast.16, bf16[2048,128]{1,0:T(8,128)(2,1)} %bitcast.17, ...), custom_call_target="tpu_custom_call" | custom-call | tf_op jit(solution)/shard_map/prefix_attention/pallas_call | solution.py:415
  63.0 0.0 copy-start
  63.0 2.3 %copy.13 = bf16[1,4,128,8,128]{4,3,2,1,0:T(8,128)(2,1)} copy(bf16[1,4,128,8,128]{4,3,2,1,0:T(8,128)(2,1)} %bitcast.15) | data formatting | bytes 2097152
  65.3 0.0 copy-done
  65.3 0.6 copy.14
Async XLA Ops:
  63.0 2.3 %copy-start = (f32[8,128]{1,0:T(8,128)S(1)}, f32[8,128]{1,0:T(8,128)}, u32[]{:S(2)}) copy-start(f32[8,128]{1,0:T(8,128)} %get-tuple-element.5) | copy-start | bytes 12292

commit v3 on v2

--- a/solution.py
+++ b/solution.py
@@ -8,9 +8,9 @@
 from jax.sharding import PartitionSpec as P
 
 MESH = pl.DeviceIdType.MESH
-SIZES = (8, 8, 8, 8, 8, 8, 8, 8)
+SIZES = (8, 8, 8, 8, 8, 8, 8, 4, 4)
 DETOUR = ()
-RELAY = ((0, 1, 2), (3, 4, 5), (6, 7), (), (), (), (), ())
+RELAY = ((0, 1, 2), (3, 4, 5), (6, 7, 8), (), (), (), (), (), ())
 AHEAD = 4
 COLS = 256
 EXTRA = 16
@@ -20,7 +20,7 @@
 VMEM_LIMIT = 60 * 1024 * 1024
 
 
-def kernel(n_dp, n_mp, q_hbm, ck_hbm, cv_hbm, pk_hbm, pv_hbm, w_hbm, count_hbm, parent_hbm, att_ref, logit_ref, *scratch):
+def kernel(n_dp, n_mp, q_hbm, ck_hbm, cv_hbm, pk_hbm, pv_hbm, w_hbm, count_hbm, parent_hbm, att_hbm, logit_ref, *scratch):
     scratch = list(scratch)
 
     def take(n):
@@ -32,7 +32,7 @@
     q_ref, ck_ref, cv_ref, w_ref, count_ref, parent_ref = take(6)
     acc_ref, m_ref, qq_ref, part_ref, gather_ref, z_ref, vt_ref, member_ref, done_ref = take(9)
     s_ref, top_ref, p_ref, alpha_ref = take(4)
-    in_sem, own_sem, recv_sem, z_sem, d2d_sem, fwd_sem, out_sem, relay_sem, pass_sem, y_send, y_recv = scratch
+    in_sem, own_sem, recv_sem, z_sem, d2d_sem, fwd_sem, out_sem, relay_sem, pass_sem, done_sem, y_send, y_recv = scratch
 
     slots, rows, size = q_ref.shape
     prefix = pk_hbm.shape[0]
@@ -94,24 +94,31 @@
         for other in others:
             pl.semaphore_signal(barrier, inc=1, device_id=(other, mp), device_id_type=MESH)
 
-    greet(mate, ahead, behind, cross)
+    greet(mate, behind)
     for step in range(1, n_mp):
         pl.semaphore_signal(barrier, inc=1, device_id=(dp, lax.rem(mp + step, n_mp)), device_id_type=MESH)
 
+    def ring_used(owner):
+        return lax.rem(owner + 2, RING) == 0 if not DETOUR else owner >= 0
+
+    relayed_to = lax.rem(z + RING - 2, RING)
+
     @pl.when(core == 0)
     def _():
-        greet(brought)
+        greet(cross)
+        pl.when(ring_used(relayed_to))(lambda: greet(brought))
 
     @pl.when(core == 1)
     def _():
-        greet(via, served_from, drop)
+        pl.when(ring_used(served))(lambda: greet(served_from))
 
     for copy in loads:
         copy.start()
     for j in range(chunks):
         for kind in (0, 1):
             own(j, kind).start()
-    pl.semaphore_wait(barrier, 4 + n_mp - 1 + 1 + 2 * core)
+    sends_via, sends_on = (core * ring_used(owner).astype(jnp.int32) for owner in (z, served))
+    pl.semaphore_wait(barrier, 2 + n_mp - 1 + core + sends_via + sends_on)
 
     def remote(src, dst, send, recv, target):
         return pltpu.make_async_remote_copy(
@@ -273,7 +280,7 @@
     def stages(c, n, values, scored, keys, causal):
         earlier = vt_ref[...]
         for b in range(blocks):
-            gather(jnp.bitwise_and(c + slots - 1, slots - 1), b, earlier)
+            gather((c + slots - 1) % slots, b, earlier)
             weigh(c, b, n)
             if keys is not None:
                 score(scored, b, keys, causal)
@@ -296,14 +303,26 @@
     order = (from_row == lax.rem(to_row, heads) * 2 + to_row // heads).astype(jnp.bfloat16)
     w_ref[...] = jnp.dot(order, w_ref[...], preferred_element_type=jnp.float32).astype(jnp.bfloat16)
 
+    head_at = lax.broadcasted_iota(jnp.int32, (heads, rows), 1) % heads
+    same = head_at == lax.broadcasted_iota(jnp.int32, (heads, rows), 0)
+
+    def out(c):
+        return pltpu.make_async_copy(done_ref.at[c], att_hbm.at[c], done_sem.at[c])
+
+    def finish(c):
+        inverse = jnp.where(c < count_ref[0], 1.0 / acc_ref[c, size : size + 1], 0.0)
+        done = (acc_ref[c, :size] * inverse).astype(jnp.bfloat16)
+        both = jnp.dot(w_ref[...], done, preferred_element_type=jnp.float32)
+        for k in (0, 1):
+            z_ref[c, k] = jnp.sum(jnp.where(same, both[k * heads : (k + 1) * heads], 0.0), axis=0, keepdims=True)
+        done_ref[c] = done.T
+        out(c).start()
+
     for b in range(blocks):
         score(0, b, ck_ref[0], True)
 
-    def own_step(c, _):
+    for c in range(slots - 1):
         stages(c, ck_ref.shape[1], cv_ref[c], c + 1, ck_ref[c + 1], True)
-        return 0
-
-    lax.fori_loop(0, slots - 1, own_step, 0)
 
     def distance(c):
         return jnp.bitwise_and(dp - parent_ref[0, c], 3)
@@ -322,12 +341,10 @@
     def compute(j):
         arrive(j)
         cross_over(j)
-
-        def one(c, _):
+        for c in range(slots - 1):
             stages(c, sizes[j], bufs[j][distance(c), 1], c + 1, bufs[j][distance(c + 1), 0], False)
-            return 0
-
-        lax.fori_loop(0, slots - 1, one, 0)
+            if j == chunks - 1 and c >= 1:
+                finish(c - 1)
 
     for j in range(chunks):
         wait_slot(j, 2)
@@ -346,23 +363,10 @@
             compute(j - 1)
     compute(chunks - 1)
     cross_over(chunks)
+    finish(slots - 2)
     for b in range(blocks):
         gather(slots - 1, b, vt_ref[...])
-
-    weight = w_ref[...]
-    head_at = lax.broadcasted_iota(jnp.int32, (heads, rows), 1) % heads
-    same = head_at == lax.broadcasted_iota(jnp.int32, (heads, rows), 0)
-
-    def last(c, _):
-        inverse = jnp.where(c < count_ref[0], 1.0 / acc_ref[c, size : size + 1], 0.0)
-        done = (acc_ref[c, :size] * inverse).astype(jnp.bfloat16)
-        done_ref[c] = done
-        both = jnp.dot(weight, done, preferred_element_type=jnp.float32)
-        for k in (0, 1):
-            z_ref[c, k] = jnp.sum(jnp.where(same, both[k * heads : (k + 1) * heads], 0.0), axis=0, keepdims=True)
-        return 0
-
-    lax.fori_loop(0, slots, last, 0)
+    finish(slots - 1)
 
     lanes = z_ref[...].reshape(2 * slots, rows)
     high = lanes.astype(jnp.bfloat16)
@@ -385,13 +389,10 @@
     for step in range(1, n_mp):
         to_peer(step).start()
 
-    def store(c, _):
-        att_ref[c] = done_ref[c].T
-        return 0
-
-    lax.fori_loop(0, slots, store, 0)
     for j in range(max(chunks - 2, 0), chunks):
         settle(j)
+    for c in range(slots):
+        out(c).wait()
     total = part_ref[...]
     for step in range(1, n_mp):
         to_peer(step).wait_recv()
@@ -419,7 +420,7 @@
                 jax.ShapeDtypeStruct((2 * slots, steps), f32),
             ),
             in_specs=[pl.BlockSpec(memory_space=pltpu.HBM)] * 8,
-            out_specs=(pl.BlockSpec(memory_space=pltpu.VMEM),) * 2,
+            out_specs=(pl.BlockSpec(memory_space=pltpu.HBM), pl.BlockSpec(memory_space=pltpu.VMEM)),
             scratch_shapes=[pltpu.VMEM((4, 2, n, size), bf16) for n in sizes]
             + [pltpu.VMEM((2, n, size), bf16) for n in sizes]
             + [
@@ -437,7 +438,7 @@
                 pltpu.VMEM((slots, 2, 1, rows), f32),
                 pltpu.VMEM((size + EXTRA, most), bf16),
                 pltpu.VMEM((rows, steps), bf16),
-                pltpu.VMEM((slots, size, rows), bf16),
+                pltpu.VMEM((slots, rows, size), bf16),
             ]
             + [
                 pltpu.VMEM((most, rows), f32),
@@ -447,6 +448,7 @@
             ]
             + [dma((6,)), dma((chunks,)), dma((3, chunks))]
             + [dma((chunks,))] * 6
+            + [dma((slots,))]
             + [dma((max(n_mp - 1, 1),))] * 2,
             compiler_params=pltpu.CompilerParams(
                 collective_id=0, has_side_effects=True, vmem_limit_bytes=VMEM_LIMIT

time: 66 us -> 56.6 us (0.86)
  the two profiles are of different devices: /device:TPU:128 before, /device:TPU:130 now
where the time goes in v3:
time: 56.6 us; the launch traced here: 56.5 us
  Pallas kernels  52.3 us (92%)
  local copies, waits for them, and re-layouts  2.86 us (5%)
  between operations  1.29 us (2%)
    pallas_call x1, Pallas kernels, step(): pl.pallas_call(functools.partial(kernel, n_dp, n_mp), out_shape=(jax.Shap...  52.3 us
    unnamed x4, local copies, waits for them, and re-layouts  2.86 us

profile of v3, /device:TPU:130, one launch (start us, length us, event | category | flops | bytes accessed | tf_op | source)
XLA Modules:
  0.0 56.5 jit_solution(11671753978605393459)
XLA Ops:
  1.3 52.3 %prefix_attention.1 = (bf16[4,1024,128]{2,1,0:T(8,128)(2,1)}, f32[8,128]{1,0:T(8,128)}) custom-call(bf16[4,1024,128]{2,1,0:T(8,128)(2,1)} %bitcast.14, bf16[4,128,128]{2,1,0:T(8,128)(2,1)} %bitcast.18, bf16[4,128,128]{2,1,0:T(8,128)(2,1)} %bitcast.19, bf16[2048,128]{1,0:T(8,128)(2,1)} %bitcast.16, bf16[2048,128]{1,0:T(8,128)(2,1)} %bitcast.17, ...), custom_call_target="tpu_custom_call" | custom-call | tf_op jit(solution)/shard_map/prefix_attention/pallas_call | solution.py:416
  53.6 0.0 copy-start
  53.6 2.3 %copy.13 = bf16[1,4,128,8,128]{4,3,2,1,0:T(8,128)(2,1)} copy(bf16[1,4,128,8,128]{4,3,2,1,0:T(8,128)(2,1)} %bitcast.15) | data formatting | bytes 2097152
  55.9 0.0 copy-done
  55.9 0.6 %copy.14 = f32[1,4,128,2]{2,3,1,0:T(2,128)} copy(f32[1,4,128,2]{2,3,1,0:T(2,128)S(1)} %bitcast.21) | data formatting | bytes 8192
Async XLA Ops:
  53.6 2.3 %copy-start = (f32[8,128]{1,0:T(8,128)S(1)}, f32[8,128]{1,0:T(8,128)}, u32[]{:S(2)}) copy-start(f32[8,128]{1,0:T(8,128)} %get-tuple-element.5) | copy-start | bytes 12292

commit v4 on v3

--- a/solution.py
+++ b/solution.py
@@ -9,9 +9,10 @@
 
 MESH = pl.DeviceIdType.MESH
 SIZES = (8, 8, 8, 8, 8, 8, 8, 4, 4)
-DETOUR = ()
-RELAY = ((0, 1, 2), (3, 4, 5), (6, 7, 8), (), (), (), (), (), ())
+DETOUR = (7, 8)
+RELAY = ((0, 1, 2), (3, 4, 5), (6,), (7, 8), (), (), (), (), ())
 AHEAD = 4
+EASE = 2
 COLS = 256
 EXTRA = 16
 RING = 8
@@ -32,7 +33,7 @@
     q_ref, ck_ref, cv_ref, w_ref, count_ref, parent_ref = take(6)
     acc_ref, m_ref, qq_ref, part_ref, gather_ref, z_ref, vt_ref, member_ref, done_ref = take(9)
     s_ref, top_ref, p_ref, alpha_ref = take(4)
-    in_sem, own_sem, recv_sem, z_sem, d2d_sem, fwd_sem, out_sem, relay_sem, pass_sem, done_sem, y_send, y_recv = scratch
+    in_sem, own_sem, recv_sem, z_sem, d2d_sem, fwd_sem, out_sem, relay_sem, pass_sem, done_sem, y_send, y_recv, via_ready, drop_ready = scratch
 
     slots, rows, size = q_ref.shape
     prefix = pk_hbm.shape[0]
@@ -102,23 +103,42 @@
         return lax.rem(owner + 2, RING) == 0 if not DETOUR else owner >= 0
 
     relayed_to = lax.rem(z + RING - 2, RING)
-
-    @pl.when(core == 0)
-    def _():
-        greet(cross)
-        pl.when(ring_used(relayed_to))(lambda: greet(brought))
-
-    @pl.when(core == 1)
-    def _():
-        pl.when(ring_used(served))(lambda: greet(served_from))
+    sends_via = jnp.logical_and(core == 1, ring_used(z))
+    passes_on = jnp.logical_and(core == 1, ring_used(served))
+    is_brought = jnp.logical_and(core == 0, ring_used(relayed_to))
+    via_late = z < 3
+    served_early = z >= RING - 3
+    drop_late = z < 3
+    brought_early = z >= RING - 3
+    no = jnp.logical_not
+
+    def both(*conditions):
+        return functools.reduce(jnp.logical_and, conditions)
+
+    pl.when(core == 0)(lambda: greet(cross))
+    pl.when(both(sends_via, via_late))(lambda: greet(via))
+    pl.when(both(passes_on, no(served_early)))(lambda: greet(served_from))
+    pl.when(both(passes_on, drop_late))(lambda: greet(drop))
+    pl.when(both(is_brought, no(brought_early)))(lambda: greet(brought))
 
     for copy in loads:
         copy.start()
     for j in range(chunks):
         for kind in (0, 1):
             own(j, kind).start()
-    sends_via, sends_on = (core * ring_used(owner).astype(jnp.int32) for owner in (z, served))
-    pl.semaphore_wait(barrier, 2 + n_mp - 1 + core + sends_via + sends_on)
+    waits_for = (
+        both(sends_via, no(via_late)),
+        both(passes_on, served_early),
+        both(passes_on, no(drop_late)),
+        both(is_brought, brought_early),
+    )
+    pl.semaphore_wait(barrier, 2 + n_mp - 1 + core + sum(w.astype(jnp.int32) for w in waits_for))
+
+    def tell(other, sem):
+        pl.semaphore_signal(sem, inc=1, device_id=(other, mp), device_id_type=MESH)
+
+    pl.when(both(passes_on, served_early))(lambda: tell(served_from, via_ready))
+    pl.when(both(is_brought, brought_early))(lambda: tell(brought, drop_ready))
 
     def remote(src, dst, send, recv, target):
         return pltpu.make_async_remote_copy(
@@ -192,8 +212,8 @@
 
         @pl.when(core == 1)
         def _():
+            off_ring(j, lax.rem(z + RING - 1, RING), lambda: two_to_next(j).start())
             two_to_mate(j, 1).start()
-            off_ring(j, lax.rem(z + RING - 1, RING), lambda: two_to_next(j).start())
 
     def settle(j):
         wait_sent(j, z_sem)
@@ -211,19 +231,18 @@
 
     start_direct(0)
 
-    @pl.when(core == 1)
-    def _():
+    def start_detours():
         for j in range(chunks):
             start_detour(j)
 
+    pl.when(both(sends_via, no(via_late)))(start_detours)
+
     for j in range(1, AHEAD):
         start_direct(j)
-    eager = lax.rem(z + 1, RING) <= 1
-
-    @pl.when(eager)
-    def _():
-        for j in range(AHEAD, chunks):
-            start_direct(j)
+    most_extra = chunks - AHEAD
+    extra = jnp.where(z == RING - 1, most_extra, jnp.maximum(most_extra - EASE * z, 0))
+    for j in range(AHEAD, chunks):
+        pl.when(extra > j - AHEAD)(functools.partial(start_direct, j))
 
     for copy in loads:
         copy.wait()
@@ -264,23 +283,19 @@
         alpha_ref[:, cols] = jnp.exp2(old - peak)
         p_ref[:n, cols] = jnp.exp2(s_ref[:n, cols] - peak).astype(jnp.bfloat16)
 
-    def gather(c, b, values):
+    def gather(c, b, n):
         cols = cols_of(b)
         acc_ref[c, :, cols] = acc_ref[c, :, cols] * alpha_ref[:, cols] + jnp.dot(
-            values, p_ref[:, cols], preferred_element_type=jnp.float32
+            vt_ref[:, :n], p_ref[:n, cols], preferred_element_type=jnp.float32
         )
 
     def keep_columns(values):
-        n = values.shape[0]
-        vt_ref[:size, :n] = values.T
-        if n < most:
-            vt_ref[:size, n:] = jnp.zeros((size, most - n), jnp.bfloat16)
-        vt_ref[size:, :] = (lax.broadcasted_iota(jnp.int32, (EXTRA, most), 1) < n).astype(jnp.bfloat16)
-
-    def stages(c, n, values, scored, keys, causal):
-        earlier = vt_ref[...]
+        vt_ref[:size, : values.shape[0]] = values.T
+
+    def stages(c, n, before, values, scored, keys, causal):
         for b in range(blocks):
-            gather((c + slots - 1) % slots, b, earlier)
+            if before:
+                gather((c + slots - 1) % slots, b, before)
             weigh(c, b, n)
             if keys is not None:
                 score(scored, b, keys, causal)
@@ -292,9 +307,7 @@
         return 0
 
     lax.fori_loop(0, slots, zero, 0)
-    vt_ref[...] = jnp.zeros(vt_ref.shape, jnp.bfloat16)
-    p_ref[...] = jnp.zeros(p_ref.shape, jnp.bfloat16)
-    alpha_ref[...] = jnp.ones(alpha_ref.shape, jnp.float32)
+    vt_ref[size:, :] = jnp.ones((EXTRA, most), jnp.bfloat16)
 
     group = lax.broadcasted_iota(jnp.int32, member_ref.shape, 0) // heads
     member_ref[...] = (group == lax.broadcasted_iota(jnp.int32, member_ref.shape, 1)).astype(jnp.bfloat16)
@@ -322,7 +335,7 @@
         score(0, b, ck_ref[0], True)
 
     for c in range(slots - 1):
-        stages(c, ck_ref.shape[1], cv_ref[c], c + 1, ck_ref[c + 1], True)
+        stages(c, ck_ref.shape[1], ck_ref.shape[1] if c else 0, cv_ref[c], c + 1, ck_ref[c + 1], True)
 
     def distance(c):
         return jnp.bitwise_and(dp - parent_ref[0, c], 3)
@@ -336,21 +349,33 @@
         end = slots - 1
         values = cv_ref[end] if j == 0 else bufs[j - 1][distance(end), 1]
         keys = None if j == chunks else bufs[j][distance(0), 0]
-        stages(end, values.shape[0], values, 0, keys, False)
+        stages(end, values.shape[0], values.shape[0], values, 0, keys, False)
 
     def compute(j):
         arrive(j)
         cross_over(j)
         for c in range(slots - 1):
-            stages(c, sizes[j], bufs[j][distance(c), 1], c + 1, bufs[j][distance(c + 1), 0], False)
+            earlier = sizes[j] if c else sizes[j - 1] if j else ck_ref.shape[1]
+            stages(c, sizes[j], earlier, bufs[j][distance(c), 1], c + 1, bufs[j][distance(c + 1), 0], False)
             if j == chunks - 1 and c >= 1:
                 finish(c - 1)
 
     for j in range(chunks):
         wait_slot(j, 2)
         forward(j)
-        if j + AHEAD < chunks:
-            pl.when(jnp.logical_not(eager))(functools.partial(start_direct, j + AHEAD))
+        for e in range(most_extra - j):
+            pl.when(extra == e)(functools.partial(start_direct, j + AHEAD + e))
+
+        if j == 0:
+
+            @pl.when(both(sends_via, via_late))
+            def _():
+                pl.semaphore_wait(via_ready, 1)
+                start_detours()
+
+            @pl.when(both(passes_on, drop_late))
+            def _():
+                pl.semaphore_wait(drop_ready, 1)
 
         @pl.when(core == 1)
         def _():
@@ -365,7 +390,7 @@
     cross_over(chunks)
     finish(slots - 2)
     for b in range(blocks):
-        gather(slots - 1, b, vt_ref[...])
+        gather(slots - 1, b, sizes[-1])
     finish(slots - 1)
 
     lanes = z_ref[...].reshape(2 * slots, rows)
@@ -386,7 +411,7 @@
             device_id_type=MESH,
         )
 
-    for step in range(1, n_mp):
+    for step in sorted(range(1, n_mp), key=lambda step: abs(2 * step - n_mp)):
         to_peer(step).start()
 
     for j in range(max(chunks - 2, 0), chunks):
@@ -400,6 +425,21 @@
     logit_ref[...] = total
     for step in range(1, n_mp):
         to_peer(step).wait_send()
+
+
+def place(att_in, logit_in, att_out, logit_out, att_ref, logit_ref, in_sem, out_sem):
+    slots = att_in.shape[0]
+    pieces = [(logit_in, logit_ref, logit_out)]
+    pieces += [(att_in.at[c], att_ref.at[c], att_out.at[c]) for c in range(slots)]
+    loads = [pltpu.make_async_copy(src, held, in_sem.at[k]) for k, (src, held, _) in enumerate(pieces)]
+    stores = [pltpu.make_async_copy(held, dst, out_sem.at[k]) for k, (_, held, dst) in enumerate(pieces)]
+    for load in loads:
+        load.start()
+    for load, store in zip(loads, stores):
+        load.wait()
+        store.start()
+    for store in stores:
+        store.wait()
 
 
 def solution(mesh):
@@ -449,7 +489,8 @@
             + [dma((6,)), dma((chunks,)), dma((3, chunks))]
             + [dma((chunks,))] * 6
             + [dma((slots,))]
-            + [dma((max(n_mp - 1, 1),))] * 2,
+            + [dma((max(n_mp - 1, 1),))] * 2
+            + [pltpu.SemaphoreType.REGULAR] * 2,
             compiler_params=pltpu.CompilerParams(
                 collective_id=0, has_side_effects=True, vmem_limit_bytes=VMEM_LIMIT
             ),
@@ -464,6 +505,24 @@
             count,
             parent,
         )
+        hbm = pl.BlockSpec(memory_space=pltpu.HBM)
+        attended, logits = pl.pallas_call(
+            place,
+            out_shape=(
+                jax.ShapeDtypeStruct((slots, rows, size), bf16),
+                jax.ShapeDtypeStruct((2 * slots, steps), f32),
+            ),
+            in_specs=[hbm] * 2,
+            out_specs=(hbm, hbm),
+            scratch_shapes=[
+                pltpu.VMEM((slots, rows, size), bf16),
+                pltpu.VMEM((2 * slots, steps), f32),
+                dma((slots + 1,)),
+                dma((slots + 1,)),
+            ],
+            compiler_params=pltpu.CompilerParams(vmem_limit_bytes=VMEM_LIMIT),
+            name="place",
+        )(attended, logits)
         attended = attended.reshape(1, slots, steps, heads, size)
         return attended, jnp.transpose(logits.reshape(slots, 2, steps), (0, 2, 1))[None]
 

time: 56.6 us -> 54.6 us (0.965)
  the two profiles are of different devices: /device:TPU:130 before, /device:TPU:256 now
where the time goes in v4:
time: 54.6 us; the launch traced here: 54.4 us
  Pallas kernels  53.2 us (97%)
  between operations  1.29 us (2%)
    pallas_call x1, Pallas kernels, step(): pl.pallas_call(functools.partial(kernel, n_dp, n_mp), out_shape=(jax.Shap...  51.2 us
    pallas_call x1, Pallas kernels, step(): pl.pallas_call(place, out_shape=(jax.ShapeDtypeStruct((slots, rows, size)...  2 us

profile of v4, /device:TPU:256, one launch (start us, length us, event | category | flops | bytes accessed | tf_op | source)
XLA Modules:
  0.0 54.4 jit_solution(5925512275868078238)
XLA Ops:
  1.3 51.2 %prefix_attention.1 = (bf16[4,1024,128]{2,1,0:T(8,128)(2,1)}, f32[8,128]{1,0:T(8,128)}) custom-call(bf16[4,1024,128]{2,1,0:T(8,128)(2,1)} %bitcast.14, bf16[4,128,128]{2,1,0:T(8,128)(2,1)} %bitcast.17, bf16[4,128,128]{2,1,0:T(8,128)(2,1)} %bitcast.18, bf16[2048,128]{1,0:T(8,128)(2,1)} %bitcast.15, bf16[2048,128]{1,0:T(8,128)(2,1)} %bitcast.16, ...), custom_call_target="tpu_custom_call" | custom-call | tf_op jit(solution)/shard_map/prefix_attention/pallas_call | solution.py:456
  52.4 2.0 %place.1 = (bf16[4,1024,128]{2,1,0:T(8,128)(2,1)}, f32[8,128]{1,0:T(8,128)}) custom-call(bf16[4,1024,128]{2,1,0:T(8,128)(2,1)} %get-tuple-element.6.att_in, f32[8,128]{1,0:T(8,128)} %get-tuple-element.7.logit_in), custom_call_target="tpu_custom_call" | custom-call | tf_op jit(solution)/shard_map/place/pallas_call | solution.py:509

commit v5 on v4

--- a/solution.py
+++ b/solution.py
@@ -9,8 +9,8 @@
 
 MESH = pl.DeviceIdType.MESH
 SIZES = (8, 8, 8, 8, 8, 8, 8, 4, 4)
-DETOUR = (7, 8)
-RELAY = ((0, 1, 2), (3, 4, 5), (6,), (7, 8), (), (), (), (), ())
+DETOUR = (6, 7, 8)
+RELAY = ((0, 1, 2), (3, 4, 5), (), (), (6, 7, 8), (), (), (), ())
 AHEAD = 4
 EASE = 2
 COLS = 256
@@ -235,7 +235,8 @@
         for j in range(chunks):
             start_detour(j)
 
-    pl.when(both(sends_via, no(via_late)))(start_detours)
+    sends_first = lax.rem(z + 2, RING) == 0
+    pl.when(both(sends_via, sends_first))(start_detours)
 
     for j in range(1, AHEAD):
         start_direct(j)
@@ -366,12 +367,11 @@
         for e in range(most_extra - j):
             pl.when(extra == e)(functools.partial(start_direct, j + AHEAD + e))
 
+        if j == 1:
+            pl.when(both(sends_via, via_late))(lambda: pl.semaphore_wait(via_ready, 1))
+            pl.when(both(sends_via, no(sends_first)))(start_detours)
+
         if j == 0:
-
-            @pl.when(both(sends_via, via_late))
-            def _():
-                pl.semaphore_wait(via_ready, 1)
-                start_detours()
 
             @pl.when(both(passes_on, drop_late))
             def _():

time: 54.6 us -> 60.5 us (1.11)
  the two profiles are of different devices: /device:TPU:256 before, /device:TPU:1 now
where the time goes in v5:
time: 60.5 us; the launch traced here: 60.3 us
  Pallas kernels  59 us (98%)
  between operations  1.29 us (2%)
    pallas_call x1, Pallas kernels, step(): pl.pallas_call(functools.partial(kernel, n_dp, n_mp), out_shape=(jax.Shap...  57 us
    pallas_call x1, Pallas kernels, step(): pl.pallas_call(place, out_shape=(jax.ShapeDtypeStruct((slots, rows, size)...  2 us

profile of v5, /device:TPU:1, one launch (start us, length us, event | category | flops | bytes accessed | tf_op | source)
XLA Modules:
  0.0 60.3 jit_solution(7781827483312677181)
XLA Ops:
  1.3 57.0 %prefix_attention.1 = (bf16[4,1024,128]{2,1,0:T(8,128)(2,1)}, f32[8,128]{1,0:T(8,128)}) custom-call(bf16[4,1024,128]{2,1,0:T(8,128)(2,1)} %bitcast.14, bf16[4,128,128]{2,1,0:T(8,128)(2,1)} %bitcast.17, bf16[4,128,128]{2,1,0:T(8,128)(2,1)} %bitcast.18, bf16[2048,128]{1,0:T(8,128)(2,1)} %bitcast.15, bf16[2048,128]{1,0:T(8,128)(2,1)} %bitcast.16, ...), custom_call_target="tpu_custom_call" | custom-call | tf_op jit(solution)/shard_map/prefix_attention/pallas_call | solution.py:456
  58.3 2.0 %place.1 = (bf16[4,1024,128]{2,1,0:T(8,128)(2,1)}, f32[8,128]{1,0:T(8,128)}) custom-call(bf16[4,1024,128]{2,1,0:T(8,128)(2,1)} %get-tuple-element.6.att_in, f32[8,128]{1,0:T(8,128)} %get-tuple-element.7.logit_in), custom_call_target="tpu_custom_call" | custom-call | tf_op jit(solution)/shard_map/place/pallas_call | solution.py:509
